TPU v7x, 128 devices: a whole 4x4x4 slice. The times are simulated.
128 devices in a mesh: row: 8 (over y_lo, x), col: 16 (over y_hi, z, core).
Axes of the slice: x: 4, y: 4 (y_hi: 2, y_lo: 2; y = y_hi * 2 + y_lo), z: 4, core: 2. Of those that a mesh axis runs over, the one named last changes fastest.
Arguments:
- row_constraints: bfloat16 [2048, 128, 128], P(('row', 'col')), may hold values from -0.5 to 0.5
- row_block: int32 [2048], P(('row', 'col')), may hold values from 0 to 15
- row_slots: int32 [2048, 2], P(('row', 'col')), may hold values from 0 to 1
- col_constraints: bfloat16 [4096, 128, 128], P(('col', 'row')), may hold values from -0.5 to 0.5
- col_block: int32 [4096], P(('col', 'row')), may hold values from 0 to 15
- col_slots: int32 [4096, 2], P(('col', 'row')), may hold values from 0 to 1
- primal_x: bfloat16 [16, 256, 256], replicated, may hold values from -0.5 to 0.5
- inverse_z: bfloat16 [16, 256, 256], replicated, may hold values from -0.5 to 0.5
Outputs:
- schur_cyclic: float32 [16, 128, 4096], P(None, 'row', 'col')
All inputs are finite; a program needn't handle non-finite values.
Results may differ from a plain program's by a relative error of at most 0.0065.
Values may be sent and summed in bfloat16 or wider, within the bound.
A program may use at most 192 MiB of HBM per device.

v0:
```python
import jax
import jax.numpy as jnp
from jax import lax
from jax.sharding import PartitionSpec as P

TB = 16


def strips_of(matrices, chosen_block, chosen_slot, block_edge):
    sections = matrices.shape[1] // block_edge
    layout = matrices.reshape(matrices.shape[0], sections, block_edge, sections, block_edge)
    layout = jnp.transpose(layout, (0, 3, 1, 2, 4)).reshape(
        matrices.shape[0] * sections, sections, block_edge, block_edge
    )
    return jnp.take(layout, chosen_block * sections + chosen_slot, axis=0)


def row_images(constraints, chosen_block, chosen_slot, inverse_z):
    strips = strips_of(inverse_z, chosen_block, chosen_slot, constraints.shape[-1])
    return jnp.einsum(
        "nrs,nbus->nbru", constraints, strips, preferred_element_type=jnp.float32
    ).astype(jnp.bfloat16)


def col_images(constraints, chosen_block, chosen_slot, primal_x):
    strips = strips_of(primal_x, chosen_block, chosen_slot, constraints.shape[-1])
    return jnp.einsum(
        "nart,ntu->naru", strips, constraints, preferred_element_type=jnp.float32
    ).astype(jnp.bfloat16)


def contract(images_rows, labels_rows, images_cols, labels_cols):
    row_count, sections = (images_rows.shape[0], images_rows.shape[1])
    col_count = images_cols.shape[0]
    flat_rows = images_rows.reshape(row_count * sections, -1)
    flat_cols = images_cols.reshape(col_count * sections, -1)
    products = lax.dot_general(
        flat_rows, flat_cols, (((1,), (1,)), ((), ())), preferred_element_type=jnp.float32
    )
    products = products.reshape(row_count, sections, col_count, sections)
    levels = jnp.arange(sections, dtype=jnp.float32)
    row_onehot = (labels_rows[:, 1:2].astype(jnp.float32) == levels[None, :]).astype(jnp.float32)
    col_onehot = (labels_cols[:, 1:2].astype(jnp.float32) == levels[None, :]).astype(jnp.float32)
    values = jnp.einsum("ibja,ia,jb->ij", products, row_onehot, col_onehot)
    matching = (
        labels_rows[:, 0:1].astype(jnp.float32) == labels_cols[:, 0].astype(jnp.float32)[None, :]
    )
    return jnp.where(matching, values, jnp.zeros_like(values))


def per_device(
    row_constraints,
    row_block,
    row_slots,
    col_constraints,
    col_block,
    col_slots,
    primal_x,
    inverse_z,
):
    own_images = row_images(row_constraints, row_block, row_slots[:, 1], inverse_z)
    own_labels = jnp.stack([row_block, row_slots[:, 0]], axis=1).astype(jnp.bfloat16)
    images_rows, labels_rows = (
        lax.all_gather(own_images, "col", axis=0, tiled=True),
        lax.all_gather(own_labels, "col", axis=0, tiled=True),
    )
    own_labels_col = jnp.stack([col_block, col_slots[:, 1], col_slots[:, 0]], axis=1).astype(
        jnp.bfloat16
    )
    raw_cols, all_labels_col = (
        lax.all_gather(col_constraints, "row", axis=0, tiled=True),
        lax.all_gather(own_labels_col, "row", axis=0, tiled=True),
    )
    label_ints_col = all_labels_col.astype(jnp.int32)
    images_cols = col_images(raw_cols, label_ints_col[:, 0], label_ints_col[:, 2], primal_x)
    labels_cols = all_labels_col[:, 0:2]
    values = contract(images_rows, labels_rows, images_cols, labels_cols)
    owners = lax.axis_size("row")
    row_count, col_count = values.shape
    groups = row_count // TB // owners
    shaped = values.reshape(groups, owners, TB, col_count)
    arrived = lax.all_to_all(shaped, "row", split_axis=1, concat_axis=0, tiled=True)
    return arrived.reshape(groups * owners, TB, col_count)


def solution(mesh):
    placed = (
        P(("row", "col"), None, None),
        P(("row", "col")),
        P(("row", "col"), None),
        P(("col", "row"), None, None),
        P(("col", "row")),
        P(("col", "row"), None),
        P(),
        P(),
    )
    return jax.shard_map(
        per_device, mesh=mesh, in_specs=placed, out_specs=P(None, "row", "col"), check_vma=False
    )
```

profile of v0, /device:TPU:1, one launch (start us, length us, event | category | flops | bytes accessed | tf_op | source)
XLA Modules:
  0.0 270.7 jit_solution(2442047108806989428)
XLA Ops:
  6.5 0.0 copy-start
  6.5 0.0 all-gather.7.cloned.1.call-start
  6.6 0.7 all-gather.7.cloned.1.call-update
  7.3 0.0 all-gather.5.cloned.1.call-start
  7.3 2.6 reshape.42
  9.9 1.9 copy.20
  11.8 0.7 compare_and_fusion
  12.5 2.3 gather_fusion
  14.8 0.0 copy-done
  14.8 0.5 fusion.17
  15.3 1.3 copy.21
  16.6 0.0 all-gather.5.cloned.1.call-update
  16.6 0.0 copy-done.3
  16.7 17.5 %all-gather.1 = bf16[8,32,3]{1,2,0:T(4,128)(2,1)S(1)} all-gather(bf16[1,32,3]{1,2,0:T(4,128)(2,1)S(1)} %maximum_bitcast_fusion), channel_id=1, replica_groups=mesh['row'=8,'col'=16] {'row'}, dimensions={0}, use_global_device_ids=true | all-gather | bytes 1728 | tf_op jit(solution)/shard_map/all_gather | solution.py:72
  34.3 0.1 reshape.72
  34.4 4.0 %reshape.44 = bf16[16,2,128,2,128]{4,3,2,1,0:T(2,128)(2,1)} reshape(bf16[16,256,256]{2,1,0:T(8,128)(2,1)} %param.14) | data formatting | bytes 4194304 | tf_op jit(solution)/shard_map/reshape | solution.py:11
  38.3 2.1 copy.22
  40.5 27.8 %all-gather = bf16[16,16,2]{1,2,0:T(2,128)(2,1)S(1)} all-gather(bf16[1,16,2]{1,2,0:T(2,128)(2,1)S(1)} %maximum_bitcast_fusion.1), channel_id=1, replica_groups=mesh['row'=8,'col'=16] {'col'}, dimensions={0}, use_global_device_ids=true | all-gather | bytes 1088 | tf_op jit(solution)/shard_map/all_gather | solution.py:65
  68.4 0.1 reshape.70
  68.4 0.1 fusion.27
  68.6 0.1 copy.42
  68.7 9.8 %gather_fusion.1 = bf16[256,2,128,128]{3,2,1,0:T(8,128)(2,1)} fusion(bf16[32,2,128,128]{3,2,1,0:T(8,128)(2,1)S(1)} %bitcast.65, s32[1024]{0:T(1024)S(1)} %pad_clamp_fusion), kind=kCustom, calls=%fused_computation.1 | custom fusion | bytes 33555456 | tf_op jit(solution)/shard_map/jit(_take)/gather | solution.py:15
  78.5 0.1 fusion.26
  78.6 25.6 %all-gather.7.cloned.1.call-done = bf16[256,128,128]{2,1,0:T(8,128)(2,1)} async-done(((bf16[32,128,128]{2,1,0:T(8,128)(2,1)}), bf16[256,128,128]{2,1,0:T(8,128)(2,1)}) %all-gather.7.cloned.1.call-update) | async-done | bytes 8388624 | tf_op jit(solution)/shard_map/all_gather | solution.py:71
  104.2 17.0 %fusion.7 = bf16[256,2,128,128]{3,2,1,0:T(8,128)(2,1)} fusion(bf16[256,2,128,128]{3,2,1,0:T(8,128)(2,1)} %gather_fusion.1, pred[256]{0:T(512)(128)(4,1)S(1)} %get-tuple-element.7, bf16[256,128,128]{2,1,0:T(8,128)(2,1)} %all-gather.7.cloned.1.call-done), kind=kOutput, calls=%fused_computation.9 | convolution fusion | flops 2164260864 | bytes 41943296 | tf_op jit(solution)/shard_map/nart,ntu->naru/dot_general | solution.py:27
  121.2 94.1 %all-gather.5.cloned.1.call-done = bf16[256,2,128,128]{3,2,1,0:T(8,128)(2,1)} async-done(((bf16[16,2,128,128]{3,2,1,0:T(8,128)(2,1)}), bf16[256,2,128,128]{3,2,1,0:T(8,128)(2,1)}) %all-gather.5.cloned.1.call-update) | async-done | bytes 16777232 | tf_op jit(solution)/shard_map/all_gather | solution.py:64
  215.3 35.1 %fusion.12 = bf16[256,2,256,2]{2,0,3,1:T(8,128)(2,1)S(1)} fusion(bf16[256,2,128,128]{3,2,1,0:T(8,128)(2,1)} %fusion.7, bf16[256,2,128,128,1]{3,2,1,0,4:T(8,128)(2,1)} %bitcast.76), kind=kOutput, calls=%fused_computation.13 | convolution fusion | flops 8589934592 | bytes 34078720 | tf_op jit(solution)/shard_map/dot_general | solution.py:37
  250.4 0.8 fusion.19
  251.1 0.7 fusion.23
  251.9 0.1 bitcast_select_fusion
  252.0 11.2 %all_to_all.15 = f32[2,8,16,256]{3,2,0,1:T(8,128)S(1)} all-to-all(f32[2,8,16,256]{3,2,0,1:T(8,128)S(1)} %copy.25), channel_id=1, replica_groups=mesh['row'=8,'col'=16] {'row'}, dimensions={1} | all-to-all | bytes 524288 | tf_op jit(solution)/shard_map/all_to_all | solution.py:82
  263.2 0.7 copy.61
  (25 shorter events, 0.2 us)
Async XLA Ops:
  6.5 8.3 %copy-start = (bf16[16,128,128]{2,1,0:T(8,128)(2,1)S(1)}, bf16[16,128,128]{2,1,0:T(8,128)(2,1)}, u32[]{:S(2)}) copy-start(bf16[16,128,128]{2,1,0:T(8,128)(2,1)} %param.8) | copy-start | bytes 1572868
  6.5 10.1 %copy-start.3 = (s32[16,2]{0,1:T(2,128)S(1)}, s32[16,2]{0,1:T(2,128)}, u32[]{:S(2)}) copy-start(s32[16,2]{0,1:T(2,128)} %param.10) | copy-start | bytes 388
  6.5 33.9 %copy-start.2 = (s32[16]{0:T(128)S(1)}, s32[16]{0:T(128)}, u32[]{:S(2)}) copy-start(s32[16]{0:T(128)} %param.9) | copy-start | bytes 196
  6.5 10.1 %copy-start.4 = (s32[32,2]{0,1:T(2,128)S(1)}, s32[32,2]{0,1:T(2,128)}, u32[]{:S(2)}) copy-start(s32[32,2]{0,1:T(2,128)} %param.13) | copy-start | bytes 772
  6.5 10.2 %copy-start.5 = (s32[32]{0:T(128)S(1)}, s32[32]{0:T(128)}, u32[]{:S(2)}) copy-start(s32[32]{0:T(128)} %param.12) | copy-start | bytes 388
  6.5 97.7 %all-gather.7.cloned.1.call-start = ((), (), s32[]{:S(2)}) async-start(), calls=%async_computation.2 | async-start | bytes 9437184 | tf_op jit(solution)/shard_map/all_gather | solution.py:71
  7.3 208.0 %all-gather.5.cloned.1.call-start = ((), (), s32[]{:S(2)}) async-start(), calls=%async_computation.1 | async-start | bytes 17825792 | tf_op jit(solution)/shard_map/all_gather | solution.py:64
  215.3 48.6 %copy-start.1 = (bf16[16,128,128]{2,1,0:T(8,128)(2,1)S(1)}, bf16[16,128,128]{2,1,0:T(8,128)(2,1)}, u32[]{:S(2)}) copy-start(bf16[16,128,128]{2,1,0:T(8,128)(2,1)} %param.8) | copy-start | bytes 1572868
Sparse Core Ops, SparseCore 0:
  9.0 95.1 all-gather.6
  106.7 108.5 all-gather.4
where the time goes:
time: 271 us
  waiting for transfers between devices  120 us (44%)
  blocking collectives  56.6 us (21%)
  matrix products  53.3 us (20%)
  local copies, waits for them, and re-layouts  25 us (9%)
  between operations  13.6 us (5%)
    all_gather x1, waiting for transfers between devices, per_device(): lax.all_gather(own_images, 'col', axis=0, tiled=True)  94.1 us
    dot_general x1, matrix products, contract(): lax.dot_general(flat_rows, flat_cols, (((1,), (1,)), ((), ())), preferred...  35.1 us
    all_gather x1, blocking collectives, per_device(): lax.all_gather(own_labels, 'col', axis=0, tiled=True)  27.8 us
    all_gather x1, waiting for transfers between devices, per_device(): lax.all_gather(col_constraints, 'row', axis=0, tiled=True)  25.6 us
    all_gather x1, blocking collectives, per_device(): lax.all_gather(own_labels_col, 'row', axis=0, tiled=True)  17.5 us
    dot_general x1, matrix products, col_images(): jnp.einsum('nart,ntu->naru', strips, constraints, preferred_element_type=...  17 us
    gather x2, local copies, waits for them, and re-layouts, strips_of(): return jnp.take(layout, chosen_block * sections + chosen_slot, axis=0)  12.1 us
    all_to_all x1, blocking collectives, per_device(): lax.all_to_all(shaped, 'row', split_axis=1, concat_axis=0, tiled=True)  11.2 us
  transfers between devices with their start and end apart: 2, of which 2 were waited for; matrix products, arithmetic and copies ran while one was open for 16% of the time, Pallas kernels for 0%

commit v1 on v0

v1 whole, which is shorter than its diff:
```python
import jax
import jax.numpy as jnp
from jax import lax
from jax.experimental import pallas as pl
from jax.experimental.pallas import tpu as pltpu
from jax.sharding import PartitionSpec as P

TB = 16
BLK = 128
S = 256
FLAT = BLK * BLK
WIDE = FLAT + 128
SLICES = 8
SL = FLAT // SLICES
OWN = 32
MESH = pl.DeviceIdType.MESH
F32 = jnp.float32
BF16 = jnp.bfloat16


def lanes_of(s):
    start = s * SL
    stop = WIDE if s == SLICES - 1 else start + SL
    return start, stop


def kernel(
    rows_in, cols_in, lab_in, x_in, w_in, out,
    rb, cb, lab, lab_s, xs, ws, mb, scr, acc, osend,
    row_send, row_recv, sib_send, sib_recv, col_send, col_recv, lab_send, lab_recv,
    out_send, out_recv, local,
):
    row, col = lax.axis_index("row"), lax.axis_index("col")
    y_lo, x = row // 4, row % 4
    y_hi, z, core = col // 8, (col // 2) % 4, col % 2
    y = y_hi * 2 + y_lo

    def dev(x_, y_, z_, core_):
        return ((y_ % 2) * 4 + x_, (y_ // 2) * 8 + z_ * 2 + core_)

    def yy(y_):
        return (y_ % 2) * 2 + y_ // 2

    yp, ym, y2 = (y + 1) % 4, (y + 3) % 4, (y + 2) % 4
    zp, zm, z2 = (z + 1) % 4, (z + 3) % 4, (z + 2) % 4
    xp, xm, x2 = (x + 1) % 4, (x + 3) % 4, (x + 2) % 4
    sibling = dev(x, y, z, 1 - core)
    dev_y = (dev(x, yp, z, core), dev(x, ym, z, core))
    dev_z = (dev(x, y, zp, core), dev(x, y, zm, core))
    dev_x = (dev(xp, y, z, core), dev(xm, y, z, core))

    barrier = pltpu.get_barrier_semaphore()
    y_other = y_hi * 2 + 1 - y_lo
    y_far = (y_other + 2) % 4
    greet = [dev(x, y_far, z, core), *dev_z, sibling]
    greet += [((row + n) % 8, col) for n in range(1, 8)]
    for d in greet:
        pl.semaphore_signal(barrier, inc=1, device_id=d, device_id_type=MESH)

    loads = [
        pltpu.make_async_copy(rows_in, rb.at[z, core, yy(y)], local.at[0]),
        pltpu.make_async_copy(cols_in, cb.at[x], local.at[1]),
        pltpu.make_async_copy(lab_in, lab.at[x], local.at[2]),
        pltpu.make_async_copy(x_in.at[:, :, pl.ds(0, BLK)], xs.at[0], local.at[3]),
        pltpu.make_async_copy(x_in.at[:, :, pl.ds(BLK, BLK)], xs.at[1], local.at[4]),
        pltpu.make_async_copy(w_in, ws, local.at[5]),
    ]
    for c in loads:
        c.start()
    pl.semaphore_wait(barrier, len(greet))

    def remote(src, dst, send, recv, to):
        return pltpu.make_async_remote_copy(
            src_ref=src, dst_ref=dst, send_sem=send, recv_sem=recv, device_id=to, device_id_type=MESH
        )

    sent = []

    def go(c):
        c.start()
        sent.append(c)
        return c

    def first(s):
        a, b = lanes_of(s)
        to = dev_y if s < 4 else dev_z
        return [
            go(remote(rows_in.at[:, a:b], rb.at[z, core, yy(y), :, a:b], row_send.at[s, n], row_recv.at[s, n], to[n]))
            for n in range(2)
        ]

    def second(s):
        a, b = lanes_of(s)
        mid = a + SL // 2
        to = dev_y if s < 4 else dev_z
        slot = [(z, yy(ym)), (z, yy(yp))] if s < 4 else [(zm, yy(y)), (zp, yy(y))]
        cut = [(a, mid), (mid, b)]
        got = []
        for n in range(2):
            (u, v), (c, d) = slot[n], cut[n]
            ref = rb.at[u, core, v, :, c:d]
            got.append(go(remote(ref, ref, row_send.at[s, 2 + n], row_recv.at[s, 2 + n], to[n])))
        return got

    def group(s, u, part=None):
        a, b = lanes_of(s)
        part = pl.ds(0, 4) if part is None else part
        if s < 4:
            return rb.at[u, core, part, :, a:b]
        return rb.at[part, core, yy(u), :, a:b]

    def third(s):
        to = dev_z if s < 4 else dev_y
        ref = group(s, z if s < 4 else y)
        return [go(remote(ref, ref, row_send.at[s, 4 + n], row_recv.at[s, 4 + n], to[n])) for n in range(2)]

    def fourth(s):
        to = dev_z if s < 4 else dev_y
        src = (zm, zp) if s < 4 else (ym, yp)
        got = []
        for n in range(2):
            ref = group(s, src[n], pl.ds(2 * n, 2))
            got.append(go(remote(ref, ref, row_send.at[s, 6 + n], row_recv.at[s, 6 + n], to[n])))
        return got

    def share(s, m):
        u = ((z, zm, zp, z2) if s < 4 else (y, ym, yp, y2))[m]
        ref = group(s, u)
        return go(remote(ref, ref, sib_send.at[s, m], sib_recv.at[s, m], sibling))

    labels = [
        go(remote(lab_in, lab.at[x], lab_send.at[n], lab_recv.at[n], dev((x + n + 1) % 4, y, z, core)))
        for n in range(3)
    ]
    order = [0, 4, 1, 5, 2, 6, 3, 7]
    w1 = {}
    for s in order:
        w1[s] = first(s)
    half = OWN // 2
    c1 = {}
    for h in range(2):
        for n in range(2):
            part = pl.ds((half * h) if n == 0 else (half * (1 - h)), half)
            c1[h, n] = go(remote(
                cols_in.at[part], cb.at[x, part], col_send.at[2 * h + n], col_recv.at[2 * h + n], dev_x[n]
            ))
    for c in loads:
        c.wait()
    acc[...] = jnp.zeros_like(acc)

    def images(xj, h):
        base = h * half

        def one(jj, carry):
            code = lab_s[xj, 0, xj * OWN + base + jj]
            k, p, q = code >> 2, (code >> 1) & 1, code & 1
            t = jnp.dot(cb[xj, base + jj], ws[k * 2 + q], preferred_element_type=F32).astype(BF16)
            m = jnp.dot(xs[p, k], t, preferred_element_type=F32)
            scr[0, pl.ds(jj, S, stride=half), :] = m[:, :BLK]
            scr[1, pl.ds(jj, S, stride=half), :] = m[:, BLK:]
            return carry

        lax.fori_loop(0, half, one, 0, unroll=4)

        def lay(r, carry):
            for a in range(2):
                for b in range(2):
                    at = pl.multiple_of((a * BLK + r) * half, half)
                    v = scr[b, pl.ds(at, half), :]
                    mb[xj, a * 2 + b, pl.ds(base, half), pl.ds(pl.multiple_of(r * BLK, BLK), BLK)] = v.astype(BF16)
            return carry

        lax.fori_loop(0, BLK, lay, 0, unroll=8)

    pairs = ((x, xm), (xp, x2))

    def contract(s, n):
        lo = s * SL
        left = rb[:, :, :, :, lo:lo + SL].reshape(8 * 64, SL)
        right = jnp.concatenate(
            [mb[xj, :, :, lo:lo + SL].reshape(4 * OWN, SL) for xj in pairs[n]], axis=0
        )
        acc[n] += lax.dot_general(left, right, (((1,), (1,)), ((), ())), preferred_element_type=F32)

    for c in labels:
        c.wait_recv()
    lab_copy = pltpu.make_async_copy(lab, lab_s, local.at[6])
    lab_copy.start()
    lab_copy.wait()

    w2, w3, w4, sh = {}, {}, {}, {}
    for s in order:
        for c in w1[s]:
            c.wait_recv()
        w2[s] = second(s)
    images(x, 0)
    for s in order:
        for c in w2[s]:
            c.wait_recv()
        w3[s] = third(s)
        sh[s, 0] = share(s, 0)
    images(x, 1)
    c2 = []
    for n in range(2):
        c1[0, n].wait_recv()
        part = pl.ds(half * n, half)
        ref = cb.at[(xm, xp)[n], part]
        c2.append(go(remote(ref, ref, col_send.at[4 + n], col_recv.at[4 + n], dev_x[n])))
    images(xm, 0)
    images(xp, 1)
    for s in order:
        for c in w3[s]:
            c.wait_recv()
        w4[s] = fourth(s)
        sh[s, 1] = share(s, 1)
        sh[s, 2] = share(s, 2)
    for n in range(2):
        c1[1, n].wait_recv()
    images(xm, 1)
    images(xp, 0)
    for c in c2:
        c.wait_recv()
    images(x2, 0)
    images(x2, 1)
    for s in order:
        for c in w4[s]:
            c.wait_recv()
        sh[s, 3] = share(s, 3)
        for m in range(4):
            sh[s, m].wait_recv()
        contract(s, 0)
        contract(s, 1)

    code = rb[:, :, :, :, FLAT:WIDE].reshape(8 * 64, 128).astype(F32).astype(jnp.int32)
    lane = lax.broadcasted_iota(jnp.int32, (1, 128), 1) // OWN
    chosen = (code & 3) == lane
    col_code = lab[0, 0:1, :] + lab[1, 0:1, :] + lab[2, 0:1, :] + lab[3, 0:1, :]
    total = jnp.zeros((8 * 64, 128), F32)
    for n in range(2):
        for m in range(2):
            v = jnp.where(chosen, acc[n, :, m * 128:(m + 1) * 128], 0.0)
            v = v + pltpu.roll(v, 64, 1)
            v = v + pltpu.roll(v, 32, 1)
            total = jnp.where(lane == pairs[n][m], v, total)
    total = jnp.where((code >> 2) == (col_code >> 2), total, 0.0)
    osend[...] = total.reshape(8, 2, 2, TB, 128)

    place = pl.ds(pl.multiple_of(y_lo * 128, 128), 128)
    keep = pltpu.make_async_copy(osend.at[row], out.at[:, x, :, :, place], local.at[7])
    keep.start()
    outs = []
    for n in range(1, 8):
        to = (row + n) % 8
        outs.append(go(remote(osend.at[to], out.at[:, x, :, :, place], out_send.at[n - 1], out_recv.at[n - 1], (to, col))))
    for c in outs:
        c.wait_recv()
    keep.wait()
    for c in sent:
        c.wait_send()


def per_device(
    row_constraints, row_block, row_slots, col_constraints, col_block, col_slots, primal_x, inverse_z
):
    n_row, n_col = row_constraints.shape[0], col_constraints.shape[0]
    row_code = (row_block * 4 + row_slots[:, 0] * 2 + row_slots[:, 1]).astype(BF16)
    rows = jnp.concatenate(
        [row_constraints.reshape(n_row, FLAT), jnp.broadcast_to(row_code[:, None], (n_row, 128))], axis=1
    )
    col_code = col_block * 4 + col_slots[:, 0] * 2 + col_slots[:, 1]
    mine = lax.axis_index("row") % 4
    lanes = jnp.arange(128, dtype=jnp.int32)
    placed = jnp.where(lanes // n_col == mine, jnp.tile(col_code, 128 // n_col), 0)
    lab = jnp.broadcast_to(placed[None, :], (8, 128))
    any_spec = pl.BlockSpec(memory_space=pl.ANY)
    dma = pltpu.SemaphoreType.DMA
    out = pl.pallas_call(
        kernel,
        out_shape=jax.ShapeDtypeStruct((2, 4, 2, TB, 256), F32),
        in_specs=[any_spec] * 5,
        out_specs=any_spec,
        scratch_shapes=[
            pltpu.VMEM((4, 2, 4, TB, WIDE), BF16),
            pltpu.VMEM((4, OWN, BLK, BLK), BF16),
            pltpu.VMEM((4, 8, 128), jnp.int32),
            pltpu.SMEM((4, 8, 128), jnp.int32),
            pltpu.VMEM((2, 16, S, BLK), BF16),
            pltpu.VMEM((32, BLK, S), BF16),
            pltpu.VMEM((4, 4, OWN, FLAT), BF16),
            pltpu.VMEM((2, S * OWN // 2, BLK), F32),
            pltpu.VMEM((2, 512, 256), F32),
            pltpu.VMEM((8, 2, 2, TB, 128), F32),
            dma((SLICES, 8)), dma((SLICES, 8)),
            dma((SLICES, 4)), dma((SLICES, 4)),
            dma((6,)), dma((6,)),
            dma((3,)), dma((3,)),
            dma((7,)), dma((7,)),
            dma((8,)),
        ],
        compiler_params=pltpu.CompilerParams(
            collective_id=0, has_side_effects=True, vmem_limit_bytes=58 * 1024 * 1024
        ),
    )(rows, col_constraints, lab, primal_x, inverse_z.reshape(32, BLK, S))
    return out.reshape(16, TB, 256)


def solution(mesh):
    placed = (
        P(("row", "col"), None, None),
        P(("row", "col")),
        P(("row", "col"), None),
        P(("col", "row"), None, None),
        P(("col", "row")),
        P(("col", "row"), None),
        P(),
        P(),
    )
    return jax.shard_map(
        per_device, mesh=mesh, in_specs=placed, out_specs=P(None, "row", "col"), check_vma=False
    )
```

time: 271 us -> 93.9 us (0.35)
  waiting for transfers between devices: 120 us -> 0 us
  Pallas kernels: 0 us -> 87.3 us
  blocking collectives: 56.6 us -> 0 us
  matrix products: 53.3 us -> 0 us
  local copies, waits for them, and re-layouts: 25 us -> 3.82 us
  between operations: 13.6 us -> 0.03 us
    all_gather x2 -> x0, waiting for transfers between devices: 120 us -> none  [the longest x1 94.1 us: per_device(): lax.all_gather(own_images, 'col', axis=0, tiled=True)]
    pallas_call x0 -> x1, Pallas kernels: none -> 87.3 us  [per_device(): pl.pallas_call(kernel, out_shape=jax.ShapeDtypeStruct((2, 4, 2, TB, 256),...]
    dot_general x4 -> x0, matrix products: 53.3 us -> none  [the longest x1 35.1 us: contract(): lax.dot_general(flat_rows, flat_cols, (((1,), (1,)), ((), ())), preferred...]
    all_gather x2 -> x0, blocking collectives: 45.4 us -> none  [the longest x1 27.8 us: per_device(): lax.all_gather(own_labels, 'col', axis=0, tiled=True)]
    gather x2 -> x0, local copies, waits for them, and re-layouts: 12.1 us -> none  [strips_of(): return jnp.take(layout, chosen_block * sections + chosen_slot, axis=0)]
    all_to_all x1 -> x0, blocking collectives: 11.2 us -> none  [per_device(): lax.all_to_all(shaped, 'row', split_axis=1, concat_axis=0, tiled=True)]
    reshape x3 -> x0, local copies, waits for them, and re-layouts: 6.53 us -> none  [the longest x2 6.51 us: strips_of(): matrices.reshape(matrices.shape[0], sections, block_edge, sections, block...]
    transpose x2 -> x0, local copies, waits for them, and re-layouts: 3.98 us -> none  [strips_of(): jnp.transpose(layout, (0, 3, 1, 2, 4))]
  transfers between devices with their start and end apart: 2 -> 0, of which waited for: 2 -> 0; matrix products, arithmetic and copies ran while one was open for 16% -> 0% of each run, Pallas kernels for 0% -> 0%
where the time goes in v1:
time: 93.9 us; the launch traced here: 92.7 us
  Pallas kernels  87.3 us (93%)
  local copies, waits for them, and re-layouts  3.82 us (4%)
  other arithmetic  1.59 us (2%)
    pallas_call x1, Pallas kernels, per_device(): pl.pallas_call(kernel, out_shape=jax.ShapeDtypeStruct((2, 4, 2, TB, 256),...  87.3 us
    unnamed x6, local copies, waits for them, and re-layouts  3.06 us

profile of v1, /device:TPU:1, one launch (start us, length us, event | category | flops | bytes accessed | tf_op | source)
XLA Modules:
  0.0 92.7 jit_solution(14156738582772557644)
XLA Ops:
  0.0 0.8 fusion
  0.8 0.0 copy-start
  0.8 0.0 copy-start.1
  0.8 0.1 broadcast_in_dim.6
  0.8 1.4 %copy.11 = bf16[2,8,128,128]{3,1,2,0:T(8,128)(2,1)S(1)} copy(bf16[2,8,128,128]{3,2,1,0:T(8,128)(2,1)} %bitcast.23) | data formatting | bytes 1048576
  2.2 0.8 pad_maximum_fusion.rows_in
  3.0 0.0 copy-done
  3.0 0.0 copy-done.1
  3.1 0.1 tile.10
  3.2 0.6 broadcast_in_dim.7.lab_in
  3.8 87.3 %shard_map.82 = f32[2,4,2,16,256]{4,3,2,1,0:T(8,128)} custom-call(bf16[16,16512]{1,0:T(8,128)(2,1)} %pad_maximum_fusion.rows_in, bf16[32,128,128]{2,1,0:T(8,128)(2,1)} %cols_in.1, s32[8,128]{1,0:T(8,128)} %broadcast_in_dim.7.lab_in, bf16[16,256,256]{2,1,0:T(8,128)(2,1)} %x_in.1, bf16[32,128,256]{2,1,0:T(8,128)(2,1)} %bitcast.20), custom_call_target="tpu_custom_call" | custom-call | tf_op jit(solution)/shard_map/pallas_call | solution.py:277
  91.0 1.7 %copy.13 = f32[16,16,256]{2,1,0:T(8,128)} copy(f32[16,16,256]{2,1,0:T(8,128)} %bitcast.22) | data formatting | bytes 524288
  (3 shorter events, 0.0 us)
Async XLA Ops:
  0.8 2.3 %copy-start = (s32[32,2]{0,1:T(2,128)S(1)}, s32[32,2]{0,1:T(2,128)}, u32[]{:S(2)}) copy-start(s32[32,2]{0,1:T(2,128)} %param.13) | copy-start | bytes 772
  0.8 2.3 %copy-start.1 = (s32[32]{0:T(128)S(1)}, s32[32]{0:T(128)}, u32[]{:S(2)}) copy-start(s32[32]{0:T(128)} %param.12) | copy-start | bytes 388

commit v2 on v1

v2 whole, which is shorter than its diff:
```python
import jax
import jax.numpy as jnp
from jax import lax
from jax.experimental import pallas as pl
from jax.experimental.pallas import tpu as pltpu
from jax.sharding import PartitionSpec as P

TB = 16
BLK = 128
S = 256
FLAT = BLK * BLK
WIDE = FLAT + 128
OWN = 32
HALF = OWN // 2
UNIT = 8
STEP = UNIT * BLK
PARTS = (2, 3, 2, 1)
PITCH = 17
MESH = pl.DeviceIdType.MESH
F32 = jnp.float32
BF16 = jnp.bfloat16


def units_of(s):
    start = (s // 4) * (BLK // UNIT // 2) + sum(PARTS[: s % 4])
    return start, start + PARTS[s % 4]


def lanes_of(s):
    first, last = units_of(s)
    return first * STEP, (WIDE if s == 7 else last * STEP)


def kernel(
    row_block, row_slots, col_block, col_slots, rows_in, cols_in, x_in, w_in, out,
    raw, rb, cb, lab, lab_s, xs, ws, mb, scr, acc, osend,
    row_send, row_recv, sib_send, sib_recv, col_send, col_recv, lab_send, lab_recv,
    out_send, out_recv, local,
):
    row, col = lax.axis_index("row"), lax.axis_index("col")
    y_lo, x = row // 4, row % 4
    y_hi, z, core = col // 8, (col // 2) % 4, col % 2
    y = y_hi * 2 + y_lo

    def dev(x_, y_, z_, core_):
        return ((y_ % 2) * 4 + x_, (y_ // 2) * 8 + z_ * 2 + core_)

    def yy(y_):
        return (y_ % 2) * 2 + y_ // 2

    yp, ym, y2 = (y + 1) % 4, (y + 3) % 4, (y + 2) % 4
    zp, zm, z2 = (z + 1) % 4, (z + 3) % 4, (z + 2) % 4
    xp, xm, x2 = (x + 1) % 4, (x + 3) % 4, (x + 2) % 4
    sibling = dev(x, y, z, 1 - core)
    dev_y = (dev(x, yp, z, core), dev(x, ym, z, core))
    dev_z = (dev(x, y, zp, core), dev(x, y, zm, core))
    dev_x = (dev(xp, y, z, core), dev(xm, y, z, core))

    barrier = pltpu.get_barrier_semaphore()
    y_other = y_hi * 2 + 1 - y_lo
    y_far = (y_other + 2) % 4
    greet = [dev(x, y_far, z, core), *dev_z, sibling]
    greet += [((row + n) % 8, col) for n in range(1, 8)]
    for d in greet:
        pl.semaphore_signal(barrier, inc=1, device_id=d, device_id_type=MESH)

    raw_load = pltpu.make_async_copy(rows_in, raw, local.at[0])
    raw_load.start()
    loads = [
        pltpu.make_async_copy(cols_in, cb.at[x], local.at[1]),
        pltpu.make_async_copy(w_in, ws, local.at[2]),
        pltpu.make_async_copy(x_in.at[:, :, pl.ds(0, BLK)], xs.at[0], local.at[3]),
        pltpu.make_async_copy(x_in.at[:, :, pl.ds(BLK, BLK)], xs.at[1], local.at[4]),
    ]
    for c in loads:
        c.start()

    sub = lax.broadcasted_iota(jnp.int32, (TB, 128), 0)
    mark = jnp.zeros((TB, 128), jnp.int32)
    for i in range(TB):
        mark = jnp.where(sub == i, row_block[i] * 4 + row_slots[0, i] * 2 + row_slots[1, i], mark)
    rb[z, core, yy(y), :, FLAT:WIDE] = mark.astype(F32).astype(BF16)
    lane = lax.broadcasted_iota(jnp.int32, (8, 128), 1) - x * OWN
    mark = jnp.zeros((8, 128), jnp.int32)
    for j in range(OWN):
        mark = jnp.where(lane == j, col_block[j] * 4 + col_slots[0, j] * 2 + col_slots[1, j], mark)
    lab[x] = mark

    raw_load.wait()
    for r in range(0, BLK, TB):
        tile = jnp.swapaxes(raw[:, r:r + TB, :], 0, 1)
        for n in range(TB):
            rb[z, core, yy(y), :, (r + n) * BLK:(r + n + 1) * BLK] = tile[n]
    pl.semaphore_wait(barrier, len(greet))

    def remote(src, dst, send, recv, to):
        return pltpu.make_async_remote_copy(
            src_ref=src, dst_ref=dst, send_sem=send, recv_sem=recv, device_id=to, device_id_type=MESH
        )

    sent = []

    def go(c):
        c.start()
        sent.append(c)
        return c

    def move(s, n, ref, to):
        return go(remote(ref, ref, row_send.at[s, n], row_recv.at[s, n], to))

    def block(s, a, b, cut):
        u, v = (b, a) if s < 4 else (a, b)
        return rb.at[u, core, yy(v), :, cut[0]:cut[1]]

    def axes(s):
        return ((y, ym, yp, y2), (z, zm, zp, z2)) if s < 4 else ((z, zm, zp, z2), (y, ym, yp, y2))

    def ways(s):
        return (dev_y, dev_z) if s < 4 else (dev_z, dev_y)

    def group(s, b, part=pl.ds(0, 4)):
        lo, hi = lanes_of(s)
        return rb.at[b, core, part, :, lo:hi] if s < 4 else rb.at[part, core, yy(b), :, lo:hi]

    w1, w2, w3, w4, sh = {}, {}, {}, {}, {}

    def first(s):
        f, g = axes(s)
        ref = block(s, f[0], g[0], lanes_of(s))
        w1[s] = [move(s, n, ref, ways(s)[0][n]) for n in range(2)]

    def second(s):
        for c in w1[s]:
            c.wait_recv()
        f, g = axes(s)
        lo, hi = lanes_of(s)
        mid = lo + PARTS[s % 4] * STEP // 2
        cut = ((lo, mid), (mid, hi))
        w2[s] = [move(s, 2 + n, block(s, f[1 + n], g[0], cut[n]), ways(s)[0][n]) for n in range(2)]

    def arrived(s):
        for c in w2[s]:
            c.wait_recv()
        share(s, 0)

    def third(s):
        ref = group(s, axes(s)[1][0])
        w3[s] = [move(s, 4 + n, ref, ways(s)[1][n]) for n in range(2)]

    def fourth(s):
        for c in w3[s]:
            c.wait_recv()
        f, g = axes(s)
        w4[s] = [move(s, 6 + n, group(s, g[1 + n], pl.ds(2 * n, 2)), ways(s)[1][n]) for n in range(2)]
        share(s, 1)
        share(s, 2)

    def last(s):
        for c in w4[s]:
            c.wait_recv()
        share(s, 3)

    def share(s, m):
        ref = group(s, axes(s)[1][m])
        sh[s, m] = go(remote(ref, ref, sib_send.at[s, m], sib_recv.at[s, m], sibling))

    c1 = {}

    def columns(h):
        for n in range(2):
            part = pl.ds((HALF * h) if n == 0 else (HALF * (1 - h)), HALF)
            c1[h, n] = go(remote(cols_in.at[part], cb.at[x, part], col_send.at[2 * h + n], col_recv.at[2 * h + n], dev_x[n]))

    def columns_far():
        for n in range(2):
            ref = cb.at[(xm, xp)[n], pl.ds(HALF * n, HALF)]
            c1[2, n] = go(remote(ref, ref, col_send.at[4 + n], col_recv.at[4 + n], dev_x[n]))

    def columns_wait(h):
        for n in range(2):
            c1[h, n].wait_recv()

    def images(xj, h, code_of):
        base = h * HALF
        batch = 8

        def some(i, carry):
            js = [i * batch + n for n in range(batch)]
            codes = [code_of(base + j) for j in js]
            ts = [
                jnp.dot(cb[xj, base + j], ws[(c >> 2) * 2 + (c & 1)], preferred_element_type=F32).astype(BF16)
                for j, c in zip(js, codes)
            ]
            ms = [jnp.dot(xs[(c >> 1) & 1, c >> 2], t, preferred_element_type=F32) for t, c in zip(ts, codes)]
            for j, m in zip(js, ms):
                scr[0, pl.ds(j, S, stride=PITCH), :] = m[:, :BLK]
                scr[1, pl.ds(j, S, stride=PITCH), :] = m[:, BLK:]
            return carry

        lax.fori_loop(0, HALF // batch, some, 0)

        def lay(g, carry):
            for a in range(2):
                at = pl.multiple_of((a * (BLK // UNIT) + g) * (UNIT * PITCH), 8)
                for b in range(2):
                    for r in range(UNIT):
                        v = scr[b, pl.ds(at + r * PITCH, HALF), :]
                        mb[xj, g, a * 2 + b, pl.ds(base, HALF), r * BLK:(r + 1) * BLK] = v.astype(BF16)
            return carry

        lax.fori_loop(0, BLK // UNIT, lay, 0, unroll=2)

    def own_code(j):
        return col_block[j] * 4 + col_slots[0, j] * 2 + col_slots[1, j]

    def code_at(xj):
        return lambda j: lab_s[xj, xj * OWN + j]

    pairs = ((x, xm), (xp, x2))
    ready = set()

    def contract(s, n, places):
        lo, hi = units_of(s)
        g = [axes(s)[1][m] for m in places]
        for m in places:
            if (s, m) not in ready:
                ready.add((s, m))
                sh[s, m].wait_recv()
        left = jnp.concatenate(
            [
                (
                    rb[b, :, :, :, lo * STEP:hi * STEP] if s < 4 else rb[:, :, yy(b), :, lo * STEP:hi * STEP]
                ).reshape(128, (hi - lo) * STEP)
                for b in g
            ],
            axis=0,
        )
        right = jnp.concatenate(
            [
                jnp.concatenate([mb[xj, u].reshape(4 * OWN, STEP) for u in range(lo, hi)], axis=1)
                for xj in pairs[n]
            ],
            axis=0,
        )
        got = lax.dot_general(left, right, (((1,), (1,)), ((), ())), preferred_element_type=F32)
        for i, b in enumerate(g):
            part = got[i * 128:(i + 1) * 128]
            if s < 4:
                acc[n, b] += part.reshape(2, 4, TB, 256)
            else:
                acc[n, :, :, yy(b)] += part.reshape(4, 2, TB, 256)

    near, far = (0, 1, 2), (3,)
    for s in (0, 4, 1, 5, 2, 6, 3, 7):
        first(s)
    labels = [
        go(remote(lab.at[x], lab.at[x], lab_send.at[n], lab_recv.at[n], dev((x + n + 1) % 4, y, z, core)))
        for n in range(3)
    ]
    columns(0)
    columns(1)
    for c in loads:
        c.wait()
    acc[...] = jnp.zeros_like(acc)
    images(x, 0, own_code)
    images(x, 1, own_code)
    for s in (0, 4, 1, 5, 2, 6, 3, 7):
        second(s)
    for s in (0, 4, 1, 5, 2, 6, 3, 7):
        arrived(s)
        third(s)
    for c in labels:
        c.wait_recv()
    lab_copy = pltpu.make_async_copy(lab.at[:, 0, :], lab_s, local.at[5])
    lab_copy.start()
    columns_wait(0)
    columns_far()
    lab_copy.wait()
    images(xm, 0, code_at(xm))
    images(xp, 1, code_at(xp))
    for s in (0, 4):
        fourth(s)
    columns_wait(1)
    images(xm, 1, code_at(xm))
    images(xp, 0, code_at(xp))
    for s in (1, 5):
        fourth(s)
    for s in (0, 4, 1, 5):
        contract(s, 0, near)
    for s in (2, 6):
        fourth(s)
    for s in (2, 6):
        contract(s, 0, near)
    for s in (3, 7):
        fourth(s)
    for s in (3, 7):
        contract(s, 0, near)
    for s in (0, 4):
        last(s)
    columns_wait(2)
    images(x2, 0, code_at(x2))
    images(x2, 1, code_at(x2))
    for s in (0, 4, 1, 5):
        contract(s, 1, near)
    for s in (1, 5):
        last(s)
    for s in (2, 6, 3, 7):
        contract(s, 1, near)
    for s in (0, 4):
        contract(s, 0, far)
        contract(s, 1, far)
    for s in (2, 6):
        last(s)
    for s in (1, 5):
        contract(s, 0, far)
        contract(s, 1, far)
    for s in (3, 7):
        last(s)
    for s in (2, 6, 3, 7):
        contract(s, 0, far)
        contract(s, 1, far)

    code = rb[:, :, :, :, FLAT:WIDE].reshape(8 * 64, 128).astype(F32).astype(jnp.int32)
    place = lax.broadcasted_iota(jnp.int32, (1, 128), 1) // OWN
    chosen = (code & 3) == place
    col_code = lab[0, 0:1, :] + lab[1, 0:1, :] + lab[2, 0:1, :] + lab[3, 0:1, :]
    total = jnp.zeros((8 * 64, 128), F32)
    for n in range(2):
        for m in range(2):
            v = jnp.where(chosen, acc[n, :, :, :, :, m * 128:(m + 1) * 128].reshape(8 * 64, 128), 0.0)
            v = v + pltpu.roll(v, 64, 1)
            v = v + pltpu.roll(v, 32, 1)
            total = jnp.where(place == pairs[n][m], v, total)
    total = jnp.where((code >> 2) == (col_code >> 2), total, 0.0)
    osend[...] = total.reshape(8, 2, 2, TB, 128)

    spot = pl.ds(pl.multiple_of(y_lo * 128, 128), 128)
    keep = pltpu.make_async_copy(osend.at[row], out.at[:, x, :, :, spot], local.at[6])
    outs = []
    for n in range(1, 8):
        to = (row + n) % 8
        outs.append(go(remote(osend.at[to], out.at[:, x, :, :, spot], out_send.at[n - 1], out_recv.at[n - 1], (to, col))))
    keep.start()
    for c in outs:
        c.wait_recv()
    keep.wait()
    for c in sent:
        c.wait_send()


def per_device(
    row_constraints, row_block, row_slots, col_constraints, col_block, col_slots, primal_x, inverse_z
):
    any_spec = pl.BlockSpec(memory_space=pl.ANY)
    smem = pl.BlockSpec(memory_space=pltpu.SMEM)
    dma = pltpu.SemaphoreType.DMA
    out = pl.pallas_call(
        kernel,
        out_shape=jax.ShapeDtypeStruct((2, 4, 2, TB, 256), F32),
        in_specs=[smem] * 4 + [any_spec] * 4,
        out_specs=any_spec,
        scratch_shapes=[
            pltpu.VMEM((TB, BLK, BLK), BF16),
            pltpu.VMEM((4, 2, 4, TB, WIDE), BF16),
            pltpu.VMEM((4, OWN, BLK, BLK), BF16),
            pltpu.VMEM((4, 8, 128), jnp.int32),
            pltpu.SMEM((4, 128), jnp.int32),
            pltpu.VMEM((2, 16, S, BLK), BF16),
            pltpu.VMEM((32, BLK, S), BF16),
            pltpu.VMEM((4, BLK // UNIT, 4, OWN, STEP), BF16),
            pltpu.VMEM((2, S * PITCH, BLK), F32),
            pltpu.VMEM((2, 4, 2, 4, TB, 256), F32),
            pltpu.VMEM((8, 2, 2, TB, 128), F32),
            dma((8, 8)), dma((8, 8)),
            dma((8, 4)), dma((8, 4)),
            dma((6,)), dma((6,)),
            dma((3,)), dma((3,)),
            dma((7,)), dma((7,)),
            dma((7,)),
        ],
        compiler_params=pltpu.CompilerParams(
            collective_id=0, has_side_effects=True, vmem_limit_bytes=58 * 1024 * 1024
        ),
    )(
        row_block, row_slots.T, col_block, col_slots.T,
        row_constraints, col_constraints, primal_x, inverse_z.reshape(32, BLK, S),
    )
    return out.reshape(16, TB, 256)


def solution(mesh):
    placed = (
        P(("row", "col"), None, None),
        P(("row", "col")),
        P(("row", "col"), None),
        P(("col", "row"), None, None),
        P(("col", "row")),
        P(("col", "row"), None),
        P(),
        P(),
    )
    return jax.shard_map(
        per_device, mesh=mesh, in_specs=placed, out_specs=P(None, "row", "col"), check_vma=False
    )
```

time: 93.9 us -> 70.8 us (0.75); the launches traced: 92.7 us -> 70.7 us
  Pallas kernels: 87.3 us -> 69 us
  local copies, waits for them, and re-layouts: 3.82 us -> 1.67 us
  other arithmetic: 1.59 us -> 0 us
    pallas_call x1, Pallas kernels: 87.3 us -> 69 us  [per_device(): pl.pallas_call(kernel, out_shape=jax.ShapeDtypeStruct((2, 4, 2, TB, 256),...]
    unnamed x6 -> x1, local copies, waits for them, and re-layouts: 3.06 us -> 1.67 us
where the time goes in v2:
time: 70.8 us; the launch traced here: 70.7 us
  Pallas kernels  69 us (97%)
  local copies, waits for them, and re-layouts  1.67 us (2%)
    pallas_call x1, Pallas kernels, per_device(): pl.pallas_call(kernel, out_shape=jax.ShapeDtypeStruct((2, 4, 2, TB, 256),...  69 us
    unnamed x1, local copies, waits for them, and re-layouts  1.67 us

profile of v2, /device:TPU:1, one launch (start us, length us, event | category | flops | bytes accessed | tf_op | source)
XLA Modules:
  0.0 70.7 jit_solution(8445822242477082518)
XLA Ops:
  0.0 69.0 %shard_map.82 = f32[2,4,2,16,256]{4,3,2,1,0:T(8,128)} custom-call(s32[16]{0:T(128)} %row_block.1, s32[2,16]{1,0:T(2,128)} %bitcast.6, s32[32]{0:T(128)} %col_block.1, s32[2,32]{1,0:T(2,128)} %bitcast.7, bf16[16,128,128]{2,1,0:T(8,128)(2,1)} %rows_in.1, bf16[32,128,128]{2,1,0:T(8,128)(2,1)} %cols_in.1, bf16[16,256,256]{2,1,0:T(8,128)(2,1)} %x_in.1, ...), custom_call_target="tpu_custom_call" | custom-call | tf_op jit(solution)/shard_map/pallas_call | solution.py:357
  69.0 1.7 %copy.10 = f32[16,16,256]{2,1,0:T(8,128)} copy(f32[16,16,256]{2,1,0:T(8,128)} %bitcast.5) | data formatting | bytes 524288

commit v3 on v2

--- a/solution.py
+++ b/solution.py
@@ -182,7 +182,7 @@
 
     def images(xj, h, code_of):
         base = h * HALF
-        batch = 8
+        batch = 16
 
         def some(i, carry):
             js = [i * batch + n for n in range(batch)]

time: 70.8 us -> 70 us (0.989)
  Pallas kernels: 69 us -> 68.2 us
    pallas_call x1, Pallas kernels: 69 us -> 68.2 us  [per_device(): pl.pallas_call(kernel, out_shape=jax.ShapeDtypeStruct((2, 4, 2, TB, 256),...]
where the time goes in v3:
time: 70 us; the launch traced here: 69.9 us
  Pallas kernels  68.2 us (97%)
  local copies, waits for them, and re-layouts  1.67 us (2%)
    pallas_call x1, Pallas kernels, per_device(): pl.pallas_call(kernel, out_shape=jax.ShapeDtypeStruct((2, 4, 2, TB, 256),...  68.2 us
    unnamed x1, local copies, waits for them, and re-layouts  1.67 us

profile of v3, /device:TPU:1, one launch (start us, length us, event | category | flops | bytes accessed | tf_op | source)
XLA Modules:
  0.0 69.9 jit_solution(7981140597863354631)
XLA Ops:
  0.0 68.2 %shard_map.82 = f32[2,4,2,16,256]{4,3,2,1,0:T(8,128)} custom-call(s32[16]{0:T(128)} %row_block.1, s32[2,16]{1,0:T(2,128)} %bitcast.6, s32[32]{0:T(128)} %col_block.1, s32[2,32]{1,0:T(2,128)} %bitcast.7, bf16[16,128,128]{2,1,0:T(8,128)(2,1)} %rows_in.1, bf16[32,128,128]{2,1,0:T(8,128)(2,1)} %cols_in.1, bf16[16,256,256]{2,1,0:T(8,128)(2,1)} %x_in.1, ...), custom_call_target="tpu_custom_call" | custom-call | tf_op jit(solution)/shard_map/pallas_call | solution.py:357
  68.2 1.7 %copy.10 = f32[16,16,256]{2,1,0:T(8,128)} copy(f32[16,16,256]{2,1,0:T(8,128)} %bitcast.5) | data formatting | bytes 524288
